TPU v7x, 32 devices: a whole 2x2x4 slice. The times are simulated.
32 devices in a mesh: wide: 16 (over z, x, core), narrow: 2 (over y).
Axes of the slice: x: 2, y: 2, z: 4, core: 2. Of those that a mesh axis runs over, the one named last changes fastest.
Arguments:
- video_q: bfloat16 [36864, 3072], P(('wide', 'narrow')), may hold values from -8 to 8
- video_k: bfloat16 [36864, 3072], P(('wide', 'narrow')), may hold values from -6 to 6
- video_v: bfloat16 [36864, 3072], P(('wide', 'narrow')), may hold values from -6 to 6
- text_q: bfloat16 [256, 3072], P(None, 'narrow'), may hold values from -8 to 8
- text_k: bfloat16 [256, 3072], P(None, 'narrow'), may hold values from -6 to 6
- text_v: bfloat16 [256, 3072], P(None, 'narrow'), may hold values from -6 to 6
- text_len: int32 [1], replicated, may hold values from 128 to 256
- win_start: int32 [96], replicated, may hold values from 0 to 1, as said below
Outputs:
- video_out: bfloat16 [36864, 3072], P(('wide', 'narrow'))
- text_out: bfloat16 [256, 3072], P(None, 'narrow')
Inputs may be any that keep to these rules, and one draw needn't show every extreme that they name: `win_start`: the window of 2 tile columns always holds the tile's own column.
All inputs are finite; a program needn't handle non-finite values.
Results may differ from a plain program's by a relative error of at most 0.0039.
Values may be sent and summed in bfloat16 or wider, within the bound.
No kernel may reach another device: no remote copies, remote signals or barrier semaphores. Data moves between devices by JAX's collectives and lax.ppermute only.
A program may use at most 384 MiB of HBM per device.

v0:
```python
import jax
import jax.numpy as jnp
from jax import lax
from jax.sharding import PartitionSpec as P

HDIM = 128
TT = 6
TH = 8
TW = 8
GW = 3
KT = 3
KW = 2
TXT = 256


def extended(cells, sides, width):
    for axis, dim in sides:
        count = lax.axis_size(axis)
        ends = count - 1
        head = lax.slice_in_dim(cells, 0, width, axis=dim)
        tail = lax.slice_in_dim(cells, cells.shape[dim] - width, cells.shape[dim], axis=dim)
        cells = jnp.concatenate(
            [
                lax.ppermute(tail, axis, [(i, (i + 1) % count) for i in range(ends)]),
                cells,
                lax.ppermute(head, axis, [((i + 1) % count, i) for i in range(ends)]),
            ],
            axis=dim,
        )
    return cells


def softmax_parts(queries, key_block, value_block, usable, score_scale):
    scores = (
        jnp.einsum("qhd,khd->hqk", queries, key_block, preferred_element_type=jnp.float32)
        * score_scale
    )
    if usable is not None:
        scores = jnp.where(usable[None, None, :], scores, -jnp.inf)
    peak = jnp.max(scores, axis=-1)
    weights = jnp.exp(scores - peak[:, :, None])
    totals = jnp.sum(weights, axis=-1)
    probs = weights.astype(jnp.bfloat16)
    accumulated = jnp.einsum("hqk,khd->qhd", probs, value_block, preferred_element_type=jnp.float32)
    return (peak, totals, accumulated)


def on_device(video_q, video_k, video_v, text_q, text_k, text_v, text_len, win_start):
    features = text_q.shape[1]
    local_heads = features // HDIM
    slab_count = lax.axis_size("wide")
    position = lax.axis_index("wide")
    slab_rows = video_q.shape[0] * lax.axis_size("narrow")
    tile_rows = TT * TH * TW
    tiles_here = slab_rows // tile_rows
    window_rows = KW * tile_rows
    reach = KT // 2
    score_scale = HDIM ** (-0.5)
    key_value = jnp.stack([video_k, video_v])
    query_set, pair_set = (
        lax.all_to_all(video_q[None], "narrow", split_axis=2, concat_axis=1, tiled=True),
        lax.all_to_all(key_value, "narrow", split_axis=2, concat_axis=1, tiled=True),
    )
    queries_all = query_set[0]
    beside_all = extended(pair_set[:, None], (("wide", 1),), reach)
    stacked = beside_all.reshape(2, KT * slab_rows, features)
    own_slab = beside_all[:, reach]
    text_pair = jnp.stack([text_k, text_v])
    text_usable = jnp.arange(TXT) < text_len[0]
    usable_parts = []
    for depth in range(KT):
        exists = (position + depth - reach >= 0) & (position + depth - reach < slab_count)
        usable_parts.append(jnp.broadcast_to(exists, (window_rows,)))
    usable = jnp.concatenate(usable_parts + [text_usable], 0)
    starts = lax.dynamic_slice_in_dim(win_start, position * tiles_here, tiles_here)

    def one_tile(entry):
        which, first_col = entry
        tile_row = which // GW
        offset = (tile_row * GW + first_col) * tile_rows
        pieces = [
            lax.dynamic_slice_in_dim(stacked, depth * slab_rows + offset, window_rows, 1)
            for depth in range(KT)
        ]
        key_block = jnp.concatenate(pieces + [text_pair], 1).reshape(2, -1, local_heads, HDIM)
        queries = lax.dynamic_slice_in_dim(queries_all, which * tile_rows, tile_rows, 0).reshape(
            tile_rows, local_heads, HDIM
        )
        peak, totals, accumulated = softmax_parts(
            queries, key_block[0], key_block[1], usable, score_scale
        )
        result = accumulated / jnp.transpose(totals)[:, :, None]
        return result.reshape(tile_rows, features).astype(jnp.bfloat16)

    attended = lax.map(one_tile, (jnp.arange(tiles_here, dtype=jnp.int32), starts))
    attended = attended.reshape(slab_rows, features)
    video_out = lax.all_to_all(attended, "narrow", split_axis=0, concat_axis=1, tiled=True)
    text_queries = text_q.reshape(TXT, local_heads, HDIM)
    slab_keys = own_slab[0].reshape(slab_rows, local_heads, HDIM)
    slab_values = own_slab[1].reshape(slab_rows, local_heads, HDIM)
    tile_peak, tile_sum, tile_acc = softmax_parts(
        text_queries, slab_keys, slab_values, None, score_scale
    )
    ceiling = lax.pmax(tile_peak, "wide")
    rescale = jnp.exp(tile_peak - ceiling)
    totals, accumulated = lax.psum(
        (rescale * tile_sum, jnp.transpose(rescale)[:, :, None] * tile_acc), "wide"
    )
    text_keys = text_k.reshape(TXT, local_heads, HDIM)
    text_values = text_v.reshape(TXT, local_heads, HDIM)
    self_peak, self_sum, self_acc = softmax_parts(
        text_queries, text_keys, text_values, text_usable, score_scale
    )
    top = jnp.maximum(ceiling, self_peak)
    video_scale = jnp.exp(ceiling - top)
    self_scale = jnp.exp(self_peak - top)
    numerator = (
        jnp.transpose(video_scale)[:, :, None] * accumulated
        + jnp.transpose(self_scale)[:, :, None] * self_acc
    )
    denominator = video_scale * totals + self_scale * self_sum
    text_out = (
        (numerator / jnp.transpose(denominator)[:, :, None])
        .reshape(TXT, features)
        .astype(jnp.bfloat16)
    )
    return (video_out, text_out)


def solution(mesh):
    in_specs = (
        P(("wide", "narrow"), None),
        P(("wide", "narrow"), None),
        P(("wide", "narrow"), None),
        P(None, "narrow"),
        P(None, "narrow"),
        P(None, "narrow"),
        P(),
        P(),
    )
    out_specs = (P(("wide", "narrow"), None), P(None, "narrow"))
    return jax.shard_map(
        on_device, mesh=mesh, in_specs=in_specs, out_specs=out_specs, check_vma=False
    )
```

profile of v0, /device:TPU:0, one launch (start us, length us, event | category | flops | bytes accessed | tf_op | source)
XLA Modules:
  0.0 1481.8 jit_solution(11503278117506258639)
XLA Ops:
  19.8 35.3 %copy.112 = bf16[2,1152,3072]{1,0,2:T(2,128)(2,1)} copy(bf16[2,1152,3072]{2,1,0:T(8,128)(2,1)} %pad_maximum_fusion.2) | data formatting | bytes 28311552 | tf_op jit(solution)/shard_map/stack | solution.py:59
  55.1 171.7 %all_to_all.49 = bf16[2,1152,3072]{1,0,2:T(2,128)(2,1)} all-to-all(bf16[2,1152,3072]{1,0,2:T(2,128)(2,1)} %copy.112), channel_id=1, replica_groups=mesh['wide'=16,'narrow'=2] {'narrow'}, dimensions={2} | all-to-all | bytes 28311552 | tf_op jit(solution)/shard_map/all_to_all | solution.py:62
  226.8 34.9 %copy.114 = bf16[2,2,1152,1536]{3,2,1,0:T(8,128)(2,1)} copy(bf16[2,2,1152,1536]{2,0,3,1:T(2,128)(2,1)} %bitcast.114) | data formatting | bytes 28311552 | tf_op jit(solution)/shard_map/all_to_all | solution.py:62
  269.4 30.0 %copy.117 = bf16[1,1152,3072]{1,0,2:T(2,128)(2,1)} copy(bf16[1,1152,3072]{2,1,0:T(8,128)(2,1)} %bitcast.133) | data formatting | bytes 14155776 | tf_op jit(solution)/shard_map/broadcast_in_dim | solution.py:61
  299.9 151.7 %reduce = bf16[3072,1152]{1,0:T(8,128)(2,1)} reduce(bf16[3072,1,1152]{2,1,0:T(2,128)(2,1)} %bitcast.117, bf16[]{:T(256)} %broadcast.27), dimensions={1}, to_apply=%bitcast.71.reduce_sub_computation | reduce | bytes 14155778
  467.4 76.5 %all-to-all-done.1 = bf16[2,2,884736]{2,1,0:T(2,128)(2,1)} async-done(((bf16[2,2,884736]{2,1,0:T(2,128)(2,1)}), bf16[2,2,884736]{2,1,0:T(2,128)(2,1)}, u32[]{:S(2)}, u32[]{:S(2)}) %all-to-all-start.1) | async-done | bytes 7077920 | tf_op jit(solution)/shard_map/all_to_all | solution.py:61
  578.9 23.9 %copy.148 = bf16[2,1152,2,1536]{1,2,3,0:T(2,128)(2,1)S(1)} copy(bf16[2,1152,2,1536]{1,0,3,2:T(2,128)(2,1)} %bitcast.115) | data formatting | bytes 28311552 | tf_op jit(solution)/shard_map/all_to_all | solution.py:62
  662.5 59.7 %pmax.7 = f32[12,256]{1,0:T(8,128)S(1)} all-reduce(f32[12,256]{1,0:T(8,128)S(1)} %get-tuple-element.189), channel_id=1, replica_groups=mesh['wide'=16,'narrow'=2] {'wide'}, use_global_device_ids=true, to_apply=%region_5.6 | all-reduce | flops 3072 | bytes 24576 | tf_op jit(solution)/shard_map/pmax | solution.py:104
  734.7 28.7 %pad_maximum_fusion.1 = bf16[2,3,2304,1536]{3,2,1,0:T(8,128)(2,1)} fusion(bf16[2,1,2304,1536]{3,2,1,0:T(8,128)(2,1)} %collective-permute-done.1, bf16[2,1,2304,1536]{3,2,1,0:T(8,128)(2,1)} %bitcast.121, bf16[2,1,2304,1536]{3,2,1,0:T(8,128)(2,1)} %collective-permute-done), kind=kLoop, calls=%fused_computation.17 | loop fusion | flops 42467328 | bytes 84934656 | tf_op jit(solution)/shard_map/concatenate | solution.py:22
  763.4 51.7 %copy.119 = bf16[2,6912,1536]{1,2,0:T(8,128)(2,1)} copy(bf16[2,6912,1536]{2,1,0:T(8,128)(2,1)} %bitcast.112) | data formatting | bytes 84934656 | tf_op jit(solution)/shard_map/while | solution.py:95
  815.0 514.9 %while.12 = (s32[]{:T(128)}, bf16[6,384,1536]{2,1,0:T(8,128)(2,1)}, s32[6]{0:T(128)S(1)}, s32[6]{0:T(128)S(1)}, bf16[2,6912,1536]{1,2,0:T(8,128)(2,1)}, /*index=...) while((s32[]{:T(128)}, bf16[6,384,1536]{2,1,0:T(8,128)(2,1)}, ...), condition=%wide.region_3.4_spmd, body=%wide.region_0.3_spmd.sunk | while | flops 6233644032 | bytes 260409872 | solution.py:95
  837.6 20.6 %fusion.67 = (f32[12,384]{1,0:T(8,128)S(1)}, f32[12,384,2560]{2,1,0:T(8,128)}) fusion(pred[2560]{0:T(1024)(128)(4,1)S(1)} %get-tuple-element.306, bf16[384,12,128]{0,2,1:T(8,128)(2,1)S(1)} %bitcast.113, bf16[2560,12,128]{0,2,1:T(8,128)(2,1)} %bitcast.110), kind=kOutput, calls=%fused_computation.2.clone.1 | convolution fusion | flops 3055283712 | bytes 56250880 | tf_op jit(solution)/shard_map/while/body/eval_jaxpr/qhd,khd->hqk/dot_general | solution.py:35
  858.1 20.4 %fusion.68 = f32[12,384]{1,0:T(8,128)S(1)} fusion(f32[12,384,2560]{2,1,0:T(8,128)} %get-tuple-element.254, f32[12,384]{1,0:T(8,128)S(1)} %get-tuple-element.255, pred[2560]{0:T(1024)(128)(4,1)S(1)} %get-tuple-element.306), kind=kLoop, calls=%fused_computation.3.clone.1 | loop fusion | flops 47181312 | bytes 47225344 | tf_op jit(solution)/shard_map/while/body/eval_jaxpr/reduce_sum | solution.py:42
  878.5 20.6 %fusion.69 = bf16[384,12,128]{0,2,1:T(8,128)(2,1)S(1)} fusion(bf16[2560,12,128]{0,2,1:T(8,128)(2,1)} %bitcast.111, f32[12,384,2560]{2,1,0:T(8,128)} %get-tuple-element.254, f32[12,384]{1,0:T(8,128)S(1)} %get-tuple-element.255, pred[2560]{0:T(1024)(128)(4,1)S(1)} %get-tuple-element.306, f32[384,12]{0,1:T(8,128)S(1)} %bitcast.137), kind=kOutput, calls=%fused_computation.9.clone.1 | convolution fusion | flops 3068264448 | bytes 56269312 | tf_op jit(solution)/shard_map/while/body/eval_jaxpr/hqk,khd->qhd/dot_general | solution.py:44
  923.4 20.6 %fusion.67 = (f32[12,384]{1,0:T(8,128)S(1)}, f32[12,384,2560]{2,1,0:T(8,128)}) fusion(pred[2560]{0:T(1024)(128)(4,1)S(1)} %get-tuple-element.306, bf16[384,12,128]{0,2,1:T(8,128)(2,1)S(1)} %bitcast.113, bf16[2560,12,128]{0,2,1:T(8,128)(2,1)} %bitcast.110), kind=kOutput, calls=%fused_computation.2.clone.1 | convolution fusion | flops 3055283712 | bytes 56250880 | tf_op jit(solution)/shard_map/while/body/eval_jaxpr/qhd,khd->hqk/dot_general | solution.py:35
  944.0 20.4 %fusion.68 = f32[12,384]{1,0:T(8,128)S(1)} fusion(f32[12,384,2560]{2,1,0:T(8,128)} %get-tuple-element.254, f32[12,384]{1,0:T(8,128)S(1)} %get-tuple-element.255, pred[2560]{0:T(1024)(128)(4,1)S(1)} %get-tuple-element.306), kind=kLoop, calls=%fused_computation.3.clone.1 | loop fusion | flops 47181312 | bytes 47225344 | tf_op jit(solution)/shard_map/while/body/eval_jaxpr/reduce_sum | solution.py:42
  964.3 20.6 %fusion.69 = bf16[384,12,128]{0,2,1:T(8,128)(2,1)S(1)} fusion(bf16[2560,12,128]{0,2,1:T(8,128)(2,1)} %bitcast.111, f32[12,384,2560]{2,1,0:T(8,128)} %get-tuple-element.254, f32[12,384]{1,0:T(8,128)S(1)} %get-tuple-element.255, pred[2560]{0:T(1024)(128)(4,1)S(1)} %get-tuple-element.306, f32[384,12]{0,1:T(8,128)S(1)} %bitcast.137), kind=kOutput, calls=%fused_computation.9.clone.1 | convolution fusion | flops 3068264448 | bytes 56269312 | tf_op jit(solution)/shard_map/while/body/eval_jaxpr/hqk,khd->qhd/dot_general | solution.py:44
  1009.2 20.6 %fusion.67 = (f32[12,384]{1,0:T(8,128)S(1)}, f32[12,384,2560]{2,1,0:T(8,128)}) fusion(pred[2560]{0:T(1024)(128)(4,1)S(1)} %get-tuple-element.306, bf16[384,12,128]{0,2,1:T(8,128)(2,1)S(1)} %bitcast.113, bf16[2560,12,128]{0,2,1:T(8,128)(2,1)} %bitcast.110), kind=kOutput, calls=%fused_computation.2.clone.1 | convolution fusion | flops 3055283712 | bytes 56250880 | tf_op jit(solution)/shard_map/while/body/eval_jaxpr/qhd,khd->hqk/dot_general | solution.py:35
  1029.8 20.4 %fusion.68 = f32[12,384]{1,0:T(8,128)S(1)} fusion(f32[12,384,2560]{2,1,0:T(8,128)} %get-tuple-element.254, f32[12,384]{1,0:T(8,128)S(1)} %get-tuple-element.255, pred[2560]{0:T(1024)(128)(4,1)S(1)} %get-tuple-element.306), kind=kLoop, calls=%fused_computation.3.clone.1 | loop fusion | flops 47181312 | bytes 47225344 | tf_op jit(solution)/shard_map/while/body/eval_jaxpr/reduce_sum | solution.py:42
  1050.1 20.6 %fusion.69 = bf16[384,12,128]{0,2,1:T(8,128)(2,1)S(1)} fusion(bf16[2560,12,128]{0,2,1:T(8,128)(2,1)} %bitcast.111, f32[12,384,2560]{2,1,0:T(8,128)} %get-tuple-element.254, f32[12,384]{1,0:T(8,128)S(1)} %get-tuple-element.255, pred[2560]{0:T(1024)(128)(4,1)S(1)} %get-tuple-element.306, f32[384,12]{0,1:T(8,128)S(1)} %bitcast.137), kind=kOutput, calls=%fused_computation.9.clone.1 | convolution fusion | flops 3068264448 | bytes 56269312 | tf_op jit(solution)/shard_map/while/body/eval_jaxpr/hqk,khd->qhd/dot_general | solution.py:44
  1095.0 20.6 %fusion.67 = (f32[12,384]{1,0:T(8,128)S(1)}, f32[12,384,2560]{2,1,0:T(8,128)}) fusion(pred[2560]{0:T(1024)(128)(4,1)S(1)} %get-tuple-element.306, bf16[384,12,128]{0,2,1:T(8,128)(2,1)S(1)} %bitcast.113, bf16[2560,12,128]{0,2,1:T(8,128)(2,1)} %bitcast.110), kind=kOutput, calls=%fused_computation.2.clone.1 | convolution fusion | flops 3055283712 | bytes 56250880 | tf_op jit(solution)/shard_map/while/body/eval_jaxpr/qhd,khd->hqk/dot_general | solution.py:35
  1115.6 20.4 %fusion.68 = f32[12,384]{1,0:T(8,128)S(1)} fusion(f32[12,384,2560]{2,1,0:T(8,128)} %get-tuple-element.254, f32[12,384]{1,0:T(8,128)S(1)} %get-tuple-element.255, pred[2560]{0:T(1024)(128)(4,1)S(1)} %get-tuple-element.306), kind=kLoop, calls=%fused_computation.3.clone.1 | loop fusion | flops 47181312 | bytes 47225344 | tf_op jit(solution)/shard_map/while/body/eval_jaxpr/reduce_sum | solution.py:42
  1136.0 20.6 %fusion.69 = bf16[384,12,128]{0,2,1:T(8,128)(2,1)S(1)} fusion(bf16[2560,12,128]{0,2,1:T(8,128)(2,1)} %bitcast.111, f32[12,384,2560]{2,1,0:T(8,128)} %get-tuple-element.254, f32[12,384]{1,0:T(8,128)S(1)} %get-tuple-element.255, pred[2560]{0:T(1024)(128)(4,1)S(1)} %get-tuple-element.306, f32[384,12]{0,1:T(8,128)S(1)} %bitcast.137), kind=kOutput, calls=%fused_computation.9.clone.1 | convolution fusion | flops 3068264448 | bytes 56269312 | tf_op jit(solution)/shard_map/while/body/eval_jaxpr/hqk,khd->qhd/dot_general | solution.py:44
  1180.9 20.6 %fusion.67 = (f32[12,384]{1,0:T(8,128)S(1)}, f32[12,384,2560]{2,1,0:T(8,128)}) fusion(pred[2560]{0:T(1024)(128)(4,1)S(1)} %get-tuple-element.306, bf16[384,12,128]{0,2,1:T(8,128)(2,1)S(1)} %bitcast.113, bf16[2560,12,128]{0,2,1:T(8,128)(2,1)} %bitcast.110), kind=kOutput, calls=%fused_computation.2.clone.1 | convolution fusion | flops 3055283712 | bytes 56250880 | tf_op jit(solution)/shard_map/while/body/eval_jaxpr/qhd,khd->hqk/dot_general | solution.py:35
  1201.4 20.4 %fusion.68 = f32[12,384]{1,0:T(8,128)S(1)} fusion(f32[12,384,2560]{2,1,0:T(8,128)} %get-tuple-element.254, f32[12,384]{1,0:T(8,128)S(1)} %get-tuple-element.255, pred[2560]{0:T(1024)(128)(4,1)S(1)} %get-tuple-element.306), kind=kLoop, calls=%fused_computation.3.clone.1 | loop fusion | flops 47181312 | bytes 47225344 | tf_op jit(solution)/shard_map/while/body/eval_jaxpr/reduce_sum | solution.py:42
  1221.8 20.6 %fusion.69 = bf16[384,12,128]{0,2,1:T(8,128)(2,1)S(1)} fusion(bf16[2560,12,128]{0,2,1:T(8,128)(2,1)} %bitcast.111, f32[12,384,2560]{2,1,0:T(8,128)} %get-tuple-element.254, f32[12,384]{1,0:T(8,128)S(1)} %get-tuple-element.255, pred[2560]{0:T(1024)(128)(4,1)S(1)} %get-tuple-element.306, f32[384,12]{0,1:T(8,128)S(1)} %bitcast.137), kind=kOutput, calls=%fused_computation.9.clone.1 | convolution fusion | flops 3068264448 | bytes 56269312 | tf_op jit(solution)/shard_map/while/body/eval_jaxpr/hqk,khd->qhd/dot_general | solution.py:44
  1266.7 20.6 %fusion.67 = (f32[12,384]{1,0:T(8,128)S(1)}, f32[12,384,2560]{2,1,0:T(8,128)}) fusion(pred[2560]{0:T(1024)(128)(4,1)S(1)} %get-tuple-element.306, bf16[384,12,128]{0,2,1:T(8,128)(2,1)S(1)} %bitcast.113, bf16[2560,12,128]{0,2,1:T(8,128)(2,1)} %bitcast.110), kind=kOutput, calls=%fused_computation.2.clone.1 | convolution fusion | flops 3055283712 | bytes 56250880 | tf_op jit(solution)/shard_map/while/body/eval_jaxpr/qhd,khd->hqk/dot_general | solution.py:35
  1287.2 20.4 %fusion.68 = f32[12,384]{1,0:T(8,128)S(1)} fusion(f32[12,384,2560]{2,1,0:T(8,128)} %get-tuple-element.254, f32[12,384]{1,0:T(8,128)S(1)} %get-tuple-element.255, pred[2560]{0:T(1024)(128)(4,1)S(1)} %get-tuple-element.306), kind=kLoop, calls=%fused_computation.3.clone.1 | loop fusion | flops 47181312 | bytes 47225344 | tf_op jit(solution)/shard_map/while/body/eval_jaxpr/reduce_sum | solution.py:42
  1307.6 20.6 %fusion.69 = bf16[384,12,128]{0,2,1:T(8,128)(2,1)S(1)} fusion(bf16[2560,12,128]{0,2,1:T(8,128)(2,1)} %bitcast.111, f32[12,384,2560]{2,1,0:T(8,128)} %get-tuple-element.254, f32[12,384]{1,0:T(8,128)S(1)} %get-tuple-element.255, pred[2560]{0:T(1024)(128)(4,1)S(1)} %get-tuple-element.306, f32[384,12]{0,1:T(8,128)S(1)} %bitcast.137), kind=kOutput, calls=%fused_computation.9.clone.1 | convolution fusion | flops 3068264448 | bytes 56269312 | tf_op jit(solution)/shard_map/while/body/eval_jaxpr/hqk,khd->qhd/dot_general | solution.py:44
  1337.0 17.6 %bitcast_multiply_fusion.1 = f32[256,12,128]{0,2,1:T(8,128)} fusion(bf16[2304,12,128]{0,2,1:T(8,128)(2,1)} %reshape_squeeze.7, f32[12,2304,256]{2,1,0:T(8,128)} %get-tuple-element.190, f32[12,256]{1,0:T(8,128)S(1)} %copy-done.4, f32[256,12]{0,1:T(8,128)S(1)} %copy-done.8), kind=kOutput, calls=%fused_computation.39 | convolution fusion | flops 1833566208 | bytes 36986880 | tf_op jit(solution)/shard_map/hqk,khd->qhd/dot_general | solution.py:44
  1357.5 57.8 %psum.15 = f32[12,256]{1,0:T(8,128)S(1)} all-reduce(f32[12,256]{1,0:T(8,128)S(1)} %copy-done.11), channel_id=1, replica_groups=mesh['wide'=16,'narrow'=2] {'wide'}, use_global_device_ids=true, to_apply=%region_9.10 | all-reduce | flops 3072 | bytes 24576 | tf_op jit(solution)/shard_map/psum | solution.py:106
  1415.4 32.6 %all-reduce.2.cloned.1.call-done = f32[256,12,128]{0,2,1:T(8,128)} async-done(((f32[256,12,128]{0,2,1:T(8,128)}), f32[256,12,128]{0,2,1:T(8,128)}) %all-reduce.2.cloned.1.call-update) | async-done | bytes 1572880 | tf_op jit(solution)/shard_map/psum | solution.py:106
  (124 shorter events, 306.3 us)
Async XLA Ops:
  261.7 473.0 %collective-permute-start = (bf16[2,1,2304,1536]{3,2,1,0:T(8,128)(2,1)}, bf16[2,1,2304,1536]{3,2,1,0:T(8,128)(2,1)}, u32[]{:S(2)}, u32[]{:S(2)}) collective-permute-start(bf16[2,1,2304,1536]{3,2,1,0:T(8,128)(2,1)} %bitcast.119), channel_id=1, source_target_pairs={{0,2},{2,4},{4,6},{6,8},{8,10},{10,12},{12,14},{14,16},{16,18},{18... | collective-permute-start | bytes 42467336 | tf_op jit(solution)/shard_map/ppermute | solution.py:24
  268.1 466.6 %collective-permute-start.1 = (bf16[2,1,2304,1536]{3,2,1,0:T(8,128)(2,1)}, bf16[2,1,2304,1536]{3,2,1,0:T(8,128)(2,1)}, u32[]{:S(2)}, u32[]{:S(2)}) collective-permute-start(bf16[2,1,2304,1536]{3,2,1,0:T(8,128)(2,1)} %bitcast.120), channel_id=1, source_target_pairs={{2,0},{4,2},{6,4},{8,6},{10,8},{12,10},{14,12},{16,14},{18,16},{20... | collective-permute-start | bytes 42467336 | tf_op jit(solution)/shard_map/ppermute | solution.py:26
  457.4 7.0 copy-start.5
  457.4 7.9 copy-start.6
  457.4 8.2 copy-start.7
  457.4 8.5 copy-start.14
  457.4 86.5 %all-to-all-start.1 = ((bf16[2,2,884736]{2,1,0:T(2,128)(2,1)}), bf16[2,2,884736]{2,1,0:T(2,128)(2,1)}, u32[]{:S(2)}, u32[]{:S(2)}) async-start(bf16[2,2,884736]{2,1,0:T(2,128)(2,1)} %reshape.84), calls=%async_computation.1 | async-start | bytes 14155776 | tf_op jit(solution)/shard_map/all_to_all | solution.py:61
  464.7 181.6 %copy-start = (bf16[256,1536]{0,1:T(8,128)(2,1)}, bf16[256,1536]{0,1:T(8,128)(2,1)S(1)}, u32[]{:S(2)}) copy-start(bf16[256,1536]{0,1:T(8,128)(2,1)S(1)} %copy.123) | copy-start | bytes 2359300
  465.6 93.9 %copy-start.1 = (bf16[256,1536]{0,1:T(8,128)(2,1)}, bf16[256,1536]{0,1:T(8,128)(2,1)S(1)}, u32[]{:S(2)}) copy-start(bf16[256,1536]{0,1:T(8,128)(2,1)S(1)} %copy.115) | copy-start | bytes 2359300
  465.9 93.6 %copy-start.2 = (bf16[256,1536]{0,1:T(8,128)(2,1)}, bf16[256,1536]{0,1:T(8,128)(2,1)S(1)}, u32[]{:S(2)}) copy-start(bf16[256,1536]{0,1:T(8,128)(2,1)S(1)} %copy.116) | copy-start | bytes 2359300
  466.0 93.5 %copy-start.12 = (pred[256]{0:T(512)(128)(4,1)}, pred[256]{0:T(512)(128)(4,1)S(1)}, u32[]{:S(2)}) copy-start(pred[256]{0:T(512)(128)(4,1)S(1)} %iota_compare_fusion) | copy-start | bytes 772
  662.5 71.6 %copy-start.3 = (f32[12,256]{1,0:T(8,128)}, f32[12,256]{1,0:T(8,128)S(1)}, u32[]{:S(2)}) copy-start(f32[12,256]{1,0:T(8,128)S(1)} %get-tuple-element.189) | copy-start | bytes 36868
  722.2 11.9 copy-start.9
  1330.0 7.0 copy-start.4
  1330.0 7.0 copy-start.8
  1330.0 123.8 %all-to-all-start.2 = ((bf16[2,1152,1536]{2,1,0:T(8,128)(2,1)}), bf16[2,1152,1536]{2,1,0:T(8,128)(2,1)}, u32[]{:S(2)}, u32[]{:S(2)}) async-start(bf16[2,1152,1536]{2,1,0:T(8,128)(2,1)} %bitcast.130), calls=%async_computation.2 | async-start | bytes 14155776 | tf_op jit(solution)/shard_map/all_to_all | solution.py:97
  1336.6 111.3 %all-reduce.2.cloned.1.call-start = ((), (), s32[]{:S(2)}) async-start(), calls=%async_computation.3 | async-start | bytes 3145728 | tf_op jit(solution)/shard_map/psum | solution.py:106
  1337.0 17.6 %copy-start.13 = (pred[256]{0:T(512)(128)(4,1)S(1)}, pred[256]{0:T(512)(128)(4,1)}, u32[]{:S(2)}) copy-start(pred[256]{0:T(512)(128)(4,1)} %copy-done.12) | copy-start | bytes 772
  1354.5 3.0 copy-start.11
  1354.6 60.8 %copy-start.10 = (f32[12,256]{1,0:T(8,128)S(1)}, f32[12,256]{1,0:T(8,128)}, u32[]{:S(2)}) copy-start(f32[12,256]{1,0:T(8,128)} %copy-done.9) | copy-start | bytes 36868
Sparse Core Ops, SparseCore 0:
  1354.7 93.1 all-reduce.1
where the time goes:
time: 1500 us; the launch traced here: 1480 us
  local copies, waits for them, and re-layouts  384 us (26%)
  other arithmetic  357 us (24%)
  blocking collectives  289 us (19%)
  matrix products  286 us (19%)
  waiting for transfers between devices  109 us (7%)
  starting transfers between devices  21.5 us (1%)
  loops' own time  19 us (1%)
  between operations  15.4 us (1%)
    all_to_all x1, blocking collectives, on_device(): lax.all_to_all(key_value, 'narrow', split_axis=2, concat_axis=1, tiled=True)  172 us
    unnamed x1, other arithmetic  152 us
    dot_general x8, matrix products, softmax_parts(): jnp.einsum('hqk,khd->qhd', probs, value_block, preferred_element_type=jnp...  145 us
    dot_general x8, matrix products, softmax_parts(): jnp.einsum('qhd,khd->hqk', queries, key_block, preferred_element_type=jnp...  142 us
    reduce_sum x8, other arithmetic, softmax_parts(): totals = jnp.sum(weights, axis=-1)  135 us
    all_to_all x1, waiting for transfers between devices, on_device(): lax.all_to_all(video_q[None], 'narrow', split_axis=2, concat_axis=1, tile...  76.5 us
    pmax x1, blocking collectives, on_device(): ceiling = lax.pmax(tile_peak, 'wide')  59.7 us
    all_to_all x2, local copies, waits for them, and re-layouts, on_device(): lax.all_to_all(key_value, 'narrow', split_axis=2, concat_axis=1, tiled=True)  58.8 us
  transfers between devices with their start and end apart: 5, of which 2 were waited for; matrix products, arithmetic and copies ran while one was open for 23% of the time, Pallas kernels for 0%

commit v1 on v0

--- a/solution.py
+++ b/solution.py
@@ -1,12 +1,17 @@
+import functools
+
 import jax
 import jax.numpy as jnp
 from jax import lax
+from jax.experimental import pallas as pl
+from jax.experimental.pallas import tpu as pltpu
 from jax.sharding import PartitionSpec as P
 
 HDIM = 128
 TT = 6
 TH = 8
 TW = 8
+GH = 2
 GW = 3
 KT = 3
 KW = 2
@@ -45,7 +50,7 @@
     return (peak, totals, accumulated)
 
 
-def on_device(video_q, video_k, video_v, text_q, text_k, text_v, text_len, win_start):
+def split_heads(video_q, video_k, video_v, text_q, text_k, text_v, text_len, win_start):
     features = text_q.shape[1]
     local_heads = features // HDIM
     slab_count = lax.axis_size("wide")
@@ -127,18 +132,185 @@
     return (video_out, text_out)
 
 
+TILE = TT * TH * TW
+WINDOW = KW * TILE
+ROW = GW * TILE
+EXP2_SCALE = HDIM**-0.5 * 1.4426950408889634
+SLOT = 2
+BY_ROWS = (((1,), (1,)), ((), ()))
+PLAIN = (((1,), (0,)), ((), ()))
+BY_COLS = (((0,), (0,)), ((), ()))
+
+
+def dot(a, b, dims):
+    return lax.dot_general(a, b, dims, preferred_element_type=jnp.float32)
+
+
+def video_kernel(info, q, k, v, before, after, text_k, text_v, _, out):
+    has_before, has_after, text_len = info[GW] == 1, info[GW + 1] == 1, info[GW + 2]
+    usable = lax.broadcasted_iota(jnp.int32, (TILE, TXT), 1) < text_len
+    for tile in range(GW):
+        rows = pl.ds(tile * TILE, TILE)
+        window = pl.ds(pl.multiple_of(info[tile] * TILE, TILE), WINDOW)
+        own = k[window, :]
+        keys = [
+            text_k[...],
+            own,
+            jnp.where(has_before, before[0, window, :], own),
+            jnp.where(has_after, after[0, window, :], own),
+        ]
+        values = [text_v[...], v[window, :], before[1, window, :], after[1, window, :]]
+        counts = [None, None, has_before, has_after]
+        queries = q[rows, :]
+        scores = [dot(queries, block, BY_ROWS) for block in keys]
+        scores[0] = jnp.where(usable, scores[0], -jnp.inf)
+        peak = functools.reduce(
+            jnp.maximum, [jnp.max(block, axis=1, keepdims=True) for block in scores]
+        )
+        total = jnp.zeros((TILE, 1), jnp.float32)
+        mixed = jnp.zeros((TILE, HDIM), jnp.float32)
+        for block, value, counted in zip(scores, values, counts):
+            weights = jnp.exp2((block - peak) * EXP2_SCALE)
+            part = jnp.sum(weights, axis=1, keepdims=True)
+            total += part if counted is None else jnp.where(counted, part, 0.0)
+            mixed += dot(weights.astype(jnp.bfloat16), value, PLAIN)
+        out[rows, :] = (mixed / total).astype(jnp.bfloat16)
+
+
+def video_slot(first, heads, info, q, k, v, before, after, text_k, text_v, out):
+    own = pl.BlockSpec((ROW, HDIM), lambda h, _: (0, first + h))
+    halo = pl.BlockSpec((2, ROW, HDIM), lambda h, _: (0, 0, h))
+    text = pl.BlockSpec((TXT, HDIM), lambda h, _: (0, first + h))
+    keys = KT * WINDOW + TXT
+    return pl.pallas_call(
+        video_kernel,
+        grid_spec=pltpu.PrefetchScalarGridSpec(
+            num_scalar_prefetch=1,
+            grid=(heads,),
+            in_specs=[own, own, own, halo, halo, text, text, pl.BlockSpec(memory_space=pl.ANY)],
+            out_specs=own,
+        ),
+        out_shape=jax.ShapeDtypeStruct(q.shape, jnp.bfloat16),
+        input_output_aliases={8: 0},
+        compiler_params=pltpu.CompilerParams(vmem_limit_bytes=48 * 2**20),
+        cost_estimate=pl.CostEstimate(
+            flops=heads * ROW * keys * HDIM * 4,
+            bytes_accessed=heads * ROW * HDIM * 16,
+            transcendentals=heads * ROW * keys,
+        ),
+        name="video_attention",
+    )(info, q, k, v, before, after, text_k, text_v, out)
+
+
+def text_kernel(info, text_q, k, v, text_k, text_v, peak, total, mixed):
+    def part(keys, values, usable):
+        scores = dot(keys, text_q[...], BY_ROWS)
+        if usable is not None:
+            scores = jnp.where(usable, scores, -jnp.inf)
+        top = jnp.max(scores, axis=0, keepdims=True)
+        weights = jnp.exp2((scores - top) * EXP2_SCALE)
+        return (
+            top,
+            jnp.sum(weights, axis=0, keepdims=True),
+            dot(values, weights.astype(jnp.bfloat16), BY_COLS),
+        )
+
+    video = part(k[...], v[...], None)
+    peak[0], total[0], mixed[0] = video
+
+    @pl.when(info[GW + 3] == 1)
+    def _():
+        usable = lax.broadcasted_iota(jnp.int32, (TXT, TXT), 0) < info[GW + 2]
+        own = part(text_k[...], text_v[...], usable)
+        top = jnp.maximum(peak[0], own[0])
+        scale = jnp.exp2((peak[0] - top) * EXP2_SCALE)
+        own_scale = jnp.exp2((own[0] - top) * EXP2_SCALE)
+        peak[0] = top
+        total[0] = scale * total[0] + own_scale * own[1]
+        mixed[0] = scale * mixed[0] + own_scale * own[2]
+
+
+def text_parts(info, text_q, k, v, text_k, text_v):
+    heads = k.shape[1] // HDIM
+    own = pl.BlockSpec((ROW, HDIM), lambda h, _: (0, h))
+    text = pl.BlockSpec((TXT, HDIM), lambda h, _: (0, h))
+    row = pl.BlockSpec((1, 1, TXT), lambda h, _: (h, 0, 0))
+    return pl.pallas_call(
+        text_kernel,
+        grid_spec=pltpu.PrefetchScalarGridSpec(
+            num_scalar_prefetch=1,
+            grid=(heads,),
+            in_specs=[text, own, own, text, text],
+            out_specs=[row, row, pl.BlockSpec((1, HDIM, TXT), lambda h, _: (h, 0, 0))],
+        ),
+        out_shape=[
+            jax.ShapeDtypeStruct((heads, 1, TXT), jnp.float32),
+            jax.ShapeDtypeStruct((heads, 1, TXT), jnp.float32),
+            jax.ShapeDtypeStruct((heads, HDIM, TXT), jnp.float32),
+        ],
+        compiler_params=pltpu.CompilerParams(vmem_limit_bytes=48 * 2**20),
+        cost_estimate=pl.CostEstimate(
+            flops=heads * ROW * TXT * HDIM * 4,
+            bytes_accessed=heads * (ROW + TXT) * HDIM * 4,
+            transcendentals=heads * ROW * TXT,
+        ),
+        name="text_attention",
+    )(info, text_q, k, v, text_k, text_v)
+
+
+def keep_rows(video_q, video_k, video_v, text_q, text_k, text_v, text_len, win_start):
+    features = video_q.shape[1]
+    heads = features // HDIM
+    count = lax.axis_size("wide")
+    frame, row = lax.axis_index("wide"), lax.axis_index("narrow")
+    forward = [(i, i + 1) for i in range(count - 1)]
+    backward = [(i + 1, i) for i in range(count - 1)]
+    starts = lax.dynamic_slice_in_dim(win_start, (frame * GH + row) * GW, GW)
+    info = jnp.concatenate(
+        [
+            starts,
+            jnp.stack([frame > 0, frame < count - 1]).astype(jnp.int32),
+            text_len,
+            ((frame == 0) & (row == 0)).astype(jnp.int32)[None],
+        ]
+    )
+    texts = lax.all_gather(
+        jnp.stack([text_q, text_k, text_v]), "narrow", axis=2, tiled=True
+    )
+    text_q, text_k, text_v = texts[0], texts[1], texts[2]
+    halos = []
+    for first in range(0, heads, SLOT):
+        columns = slice(first * HDIM, (first + SLOT) * HDIM)
+        pair = jnp.stack([video_k[:, columns], video_v[:, columns]])
+        halos.append(
+            (lax.ppermute(pair, "wide", forward), lax.ppermute(pair, "wide", backward))
+        )
+    peak, total, mixed = text_parts(info, text_q, video_k, video_v, text_k, text_v)
+    top = lax.pmax(peak, ("wide", "narrow"))
+    scale = jnp.exp2((peak - top) * EXP2_SCALE)
+    total, mixed = lax.psum_scatter(
+        (scale * total, scale * mixed), "narrow", scatter_dimension=0, tiled=True
+    )
+    total, mixed = lax.psum((total, mixed), "wide")
+    text_out = (
+        jnp.transpose(mixed / total, (2, 0, 1)).reshape(TXT, -1).astype(jnp.bfloat16)
+    )
+    out = jnp.zeros(video_q.shape, jnp.bfloat16)
+    for slot, (before, after) in enumerate(halos):
+        out = video_slot(
+            slot * SLOT, SLOT, info, video_q, video_k, video_v, before, after, text_k, text_v, out
+        )
+    return out, text_out
+
+
 def solution(mesh):
-    in_specs = (
-        P(("wide", "narrow"), None),
-        P(("wide", "narrow"), None),
-        P(("wide", "narrow"), None),
-        P(None, "narrow"),
-        P(None, "narrow"),
-        P(None, "narrow"),
-        P(),
-        P(),
-    )
-    out_specs = (P(("wide", "narrow"), None), P(None, "narrow"))
+    tokens = P(("wide", "narrow"), None)
+    text = P(None, "narrow")
+    body = keep_rows if mesh.shape["narrow"] == GH else split_heads
     return jax.shard_map(
-        on_device, mesh=mesh, in_specs=in_specs, out_specs=out_specs, check_vma=False
-    )
+        body,
+        mesh=mesh,
+        in_specs=(tokens, tokens, tokens, text, text, text, P(), P()),
+        out_specs=(tokens, text),
+        check_vma=False,
+    )

time: 1500 us -> 679 us (0.45)
  local copies, waits for them, and re-layouts: 384 us -> 26.5 us
  other arithmetic: 357 us -> 21.2 us
  matrix products: 286 us -> 0 us
  Pallas kernels: 0 us -> 186 us
  starting transfers between devices: 21.5 us -> 177 us
  blocking collectives: 289 us -> 139 us
  loops' own time: 19 us -> 0 us
    dot_general x16 -> x0, matrix products: 286 us -> none  [the longest x8 145 us: softmax_parts(): jnp.einsum('hqk,khd->qhd', probs, value_block, preferred_element_type=jnp...]
    pallas_call x0 -> x13, Pallas kernels: none -> 186 us  [the longest x12 150 us: video_slot(): pl.pallas_call(video_kernel, grid_spec=pltpu.PrefetchScalarGridSpec(num_s...]
    all_to_all x1 -> x0, blocking collectives: 172 us -> none  [on_device(): lax.all_to_all(key_value, 'narrow', split_axis=2, concat_axis=1, tiled=True)]
    ppermute x2 -> x24, starting transfers between devices: 7.64 us -> 177 us  [the longest x12 161 us: keep_rows(): lax.ppermute(pair, 'wide', forward)]
    unnamed x1 -> x0, other arithmetic: 152 us -> none
    reduce_sum x8 -> x0, other arithmetic: 135 us -> none  [softmax_parts(): totals = jnp.sum(weights, axis=-1)]
    all_to_all x4 -> x0, local copies, waits for them, and re-layouts: 79.6 us -> none  [the longest x2 58.8 us: on_device(): lax.all_to_all(key_value, 'narrow', split_axis=2, concat_axis=1, tiled=True)]
    all_to_all x2 -> x0, waiting for transfers between devices: 76.5 us -> none  [the longest x1 76.5 us: on_device(): lax.all_to_all(video_q[None], 'narrow', split_axis=2, concat_axis=1, tile...]
  transfers between devices with their start and end apart: 5 -> 27, of which waited for: 2 -> 2; matrix products, arithmetic and copies ran while one was open for 23% -> 4% of each run, Pallas kernels for 0% -> 22%
where the time goes in v1:
time: 679 us; the launch traced here: 671 us
  Pallas kernels  186 us (27%)
  starting transfers between devices  177 us (26%)
  blocking collectives  139 us (20%)
  waiting for transfers between devices  105 us (15%)
  local copies, waits for them, and re-layouts  26.5 us (4%)
  other arithmetic  21.2 us (3%)
  between operations  16.2 us (2%)
    ppermute x12, starting transfers between devices, keep_rows(): lax.ppermute(pair, 'wide', forward)  161 us
    pallas_call x12, Pallas kernels, video_slot(): pl.pallas_call(video_kernel, grid_spec=pltpu.PrefetchScalarGridSpec(num_s...  150 us
    psum x1, blocking collectives, keep_rows(): total, mixed = lax.psum((total, mixed), 'wide')  94.9 us
    psum x1, waiting for transfers between devices, keep_rows(): total, mixed = lax.psum((total, mixed), 'wide')  53.6 us
    all_gather x1, waiting for transfers between devices, keep_rows(): lax.all_gather(jnp.stack([text_q, text_k, text_v]), 'narrow', axis=2, til...  51.6 us
    pmax x1, blocking collectives, keep_rows(): top = lax.pmax(peak, ('wide', 'narrow'))  37 us
    pallas_call x1, Pallas kernels, text_parts(): pl.pallas_call(text_kernel, grid_spec=pltpu.PrefetchScalarGridSpec(num_sc...  35.7 us
    ppermute x12, starting transfers between devices, keep_rows(): lax.ppermute(pair, 'wide', backward)  15.7 us
  transfers between devices with their start and end apart: 27, of which 2 were waited for; matrix products, arithmetic and copies ran while one was open for 4% of the time, Pallas kernels for 22%

profile of v1, /device:TPU:0, one launch (start us, length us, event | category | flops | bytes accessed | tf_op | source)
XLA Modules:
  0.0 671.2 jit_solution(2666685886072944323)
XLA Ops:
  11.5 6.0 slice_bitcast_fusion.4
  17.5 6.9 %slice_bitcast_fusion.3 = (bf16[1,1152,256]{2,1,0:T(8,128)(2,1)}, bf16[1,1152,256]{2,1,0:T(8,128)(2,1)}, bf16[1,1152,256]{2,1,0:T(8,128)(2,1)}, bf16[1,1152,256]...) fusion(bf16[1152,3072]{1,0:T(8,128)(2,1)} %v.25), kind=kLoop, calls=%fused_computation.18 | loop fusion | bytes 14155776 | tf_op jit(solution)/shard_map/stack | solution.py:284
  24.4 51.6 %all-gather.2.cloned.1.call-done = bf16[3,256,3072]{2,1,0:T(8,128)(2,1)} async-done(((bf16[3,256,1536]{2,1,0:T(8,128)(2,1)}), bf16[3,256,3072]{2,1,0:T(8,128)(2,1)}) %all-gather.2.cloned.1.call-update) | async-done | bytes 4718608 | tf_op jit(solution)/shard_map/all_gather | solution.py:277
  78.7 35.7 %text_attention.1 = (f32[24,1,256]{2,1,0:T(1,128)S(1)}, f32[24,1,256]{2,1,0:T(1,128)S(1)}, f32[24,128,256]{2,1,0:T(8,128)}) custom-call(s32[7]{0:T(128)S(1)} %pad_add_fusion.info, bf16[256,3072]{1,0:T(8,128)(2,1)S(1)} %get-tuple-element.38.text_q, bf16[1152,3072]{1,0:T(8,128)(2,1)} %k.25, bf16[1152,3072]{1,0:T(8,128)(2,1)} %v.25, ...), custom_call_target="tpu_custom_call" | custom-call | flops 3623878656 | bytes 17301504 | tf_op jit(solution)/shard_map/text_attention/pallas_call | solution.py:238
  114.4 37.0 %pmax.7 = f32[24,1,256]{2,1,0:T(1,128)S(1)} all-reduce(f32[24,1,256]{2,1,0:T(1,128)S(1)} %get-tuple-element.5), channel_id=1, replica_groups=mesh['wide'=16,'narrow'=2] {'wide','narrow'}, use_global_device_ids=true, to_apply=%region_0.0 | all-reduce | flops 6144 | bytes 49152 | tf_op jit(solution)/shard_map/pmax | solution.py:289
  151.5 3.9 broadcast_multiply_fusion
  159.8 5.7 collective-permute-start.20
  166.9 4.4 collective-permute-start.18
  174.8 43.4 %collective-permute-start.16 = (bf16[2,1152,256]{2,1,0:T(8,128)(2,1)S(1)}, bf16[2,1152,256]{2,1,0:T(8,128)(2,1)S(1)}, u32[]{:S(2)}, u32[]{:S(2)}) collective-permute-start(bf16[2,1152,256]{2,1,0:T(8,128)(2,1)S(1)} %pad_maximum_fusion.9), channel_id=1, source_target_pairs={{0,2},{2,4},{4,6},{6,8},{8,10},{10,12},{12,14},{14,16},{16,18},{18... | collective-permute-start | bytes 3538952 | tf_op jit(solution)/shard_map/ppermute | solution.py:286
  220.7 8.1 %collective-permute-start.14 = (bf16[2,1152,256]{2,1,0:T(8,128)(2,1)}, bf16[2,1152,256]{2,1,0:T(8,128)(2,1)S(1)}, u32[]{:S(2)}, u32[]{:S(2)}) collective-permute-start(bf16[2,1152,256]{2,1,0:T(8,128)(2,1)} %pad_maximum_fusion.8), channel_id=1, source_target_pairs={{0,2},{2,4},{4,6},{6,8},{8,10},{10,12},{12,14},{14,16},{16,18},{18... | collective-permute-start | bytes 3538952 | tf_op jit(solution)/shard_map/ppermute | solution.py:286
  234.1 22.1 %collective-permute-start.12 = (bf16[2,1152,256]{2,1,0:T(8,128)(2,1)}, bf16[2,1152,256]{2,1,0:T(8,128)(2,1)}, u32[]{:S(2)}, u32[]{:S(2)}) collective-permute-start(bf16[2,1152,256]{2,1,0:T(8,128)(2,1)} %pad_maximum_fusion.7), channel_id=1, source_target_pairs={{0,2},{2,4},{4,6},{6,8},{8,10},{10,12},{12,14},{14,16},{16,18},{18... | collective-permute-start | bytes 3538952 | tf_op jit(solution)/shard_map/ppermute | solution.py:286
  258.7 35.5 %collective-permute-start.10 = (bf16[2,1152,256]{2,1,0:T(8,128)(2,1)}, bf16[2,1152,256]{2,1,0:T(8,128)(2,1)}, u32[]{:S(2)}, u32[]{:S(2)}) collective-permute-start(bf16[2,1152,256]{2,1,0:T(8,128)(2,1)} %pad_maximum_fusion.6), channel_id=1, source_target_pairs={{0,2},{2,4},{4,6},{6,8},{8,10},{10,12},{12,14},{14,16},{16,18},{18... | collective-permute-start | bytes 3538952 | tf_op jit(solution)/shard_map/ppermute | solution.py:286
  301.6 23.2 %collective-permute-start.8 = (bf16[2,1152,256]{2,1,0:T(8,128)(2,1)}, bf16[2,1152,256]{2,1,0:T(8,128)(2,1)}, u32[]{:S(2)}, u32[]{:S(2)}) collective-permute-start(bf16[2,1152,256]{2,1,0:T(8,128)(2,1)} %pad_maximum_fusion.5), channel_id=1, source_target_pairs={{0,2},{2,4},{4,6},{6,8},{8,10},{10,12},{12,14},{14,16},{16,18},{18... | collective-permute-start | bytes 3538952 | tf_op jit(solution)/shard_map/ppermute | solution.py:286
  328.6 12.3 %video_attention.12._ = bf16[1152,3072]{1,0:T(8,128)(2,1)} custom-call(s32[7]{0:T(128)S(1)} %pad_add_fusion.info, bf16[1152,3072]{1,0:T(8,128)(2,1)} %q.23, bf16[1152,3072]{1,0:T(8,128)(2,1)} %k.25, bf16[1152,3072]{1,0:T(8,128)(2,1)} %v.25, bf16[2,1152,256]{2,1,0:T(8,128)(2,1)S(1)} %copy-done.11, ...), custom_call_target="tpu_custom_call", output_to_operand_aliasing={{}: (8, {})} | custom-call | flops 3019898880 | bytes 4718592 | tf_op jit(solution)/shard_map/video_attention/pallas_call | solution.py:185
  342.4 5.1 collective-permute-start.6
  347.5 12.2 %video_attention.13._ = bf16[1152,3072]{1,0:T(8,128)(2,1)} custom-call(s32[7]{0:T(128)S(1)} %pad_add_fusion.info, bf16[1152,3072]{1,0:T(8,128)(2,1)} %q.23, bf16[1152,3072]{1,0:T(8,128)(2,1)} %k.25, bf16[1152,3072]{1,0:T(8,128)(2,1)} %v.25, bf16[2,1152,256]{2,1,0:T(8,128)(2,1)S(1)} %copy-done.3, ...), custom_call_target="tpu_custom_call", output_to_operand_aliasing={{}: (8, {})} | custom-call | flops 3019898880 | bytes 4718592 | tf_op jit(solution)/shard_map/video_attention/pallas_call | solution.py:185
  360.9 4.6 collective-permute-start.4
  365.5 12.2 %video_attention.14._ = bf16[1152,3072]{1,0:T(8,128)(2,1)} custom-call(s32[7]{0:T(128)S(1)} %pad_add_fusion.info, bf16[1152,3072]{1,0:T(8,128)(2,1)} %q.23, bf16[1152,3072]{1,0:T(8,128)(2,1)} %k.25, bf16[1152,3072]{1,0:T(8,128)(2,1)} %v.25, bf16[2,1152,256]{2,1,0:T(8,128)(2,1)S(1)} %copy-done.1, ...), custom_call_target="tpu_custom_call", output_to_operand_aliasing={{}: (8, {})} | custom-call | flops 3019898880 | bytes 4718592 | tf_op jit(solution)/shard_map/video_attention/pallas_call | solution.py:185
  377.7 6.9 %all-reduce = f32[24,1,256]{2,1,0:T(1,128)S(1)} all-reduce(f32[24,1,256]{2,1,0:T(1,128)S(1)} %get-tuple-element.12), channel_id=3, replica_groups=mesh['wide'=16,'narrow'=2] {'narrow'}, use_global_device_ids=true, to_apply=%region_3.0.clone | all-reduce | flops 6144 | bytes 49152
  387.2 12.2 %video_attention.15._ = bf16[1152,3072]{1,0:T(8,128)(2,1)} custom-call(s32[7]{0:T(128)S(1)} %pad_add_fusion.info, bf16[1152,3072]{1,0:T(8,128)(2,1)} %q.23, bf16[1152,3072]{1,0:T(8,128)(2,1)} %k.25, bf16[1152,3072]{1,0:T(8,128)(2,1)} %v.25, bf16[2,1152,256]{2,1,0:T(8,128)(2,1)S(1)} %copy-done.9, ...), custom_call_target="tpu_custom_call", output_to_operand_aliasing={{}: (8, {})} | custom-call | flops 3019898880 | bytes 4718592 | tf_op jit(solution)/shard_map/video_attention/pallas_call | solution.py:185
  399.3 12.4 %video_attention.16._ = bf16[1152,3072]{1,0:T(8,128)(2,1)} custom-call(s32[7]{0:T(128)S(1)} %pad_add_fusion.info, bf16[1152,3072]{1,0:T(8,128)(2,1)} %q.23, bf16[1152,3072]{1,0:T(8,128)(2,1)} %k.25, bf16[1152,3072]{1,0:T(8,128)(2,1)} %v.25, bf16[2,1152,256]{2,1,0:T(8,128)(2,1)S(1)} %copy-done.17, ...), custom_call_target="tpu_custom_call", output_to_operand_aliasing={{}: (8, {})} | custom-call | flops 3019898880 | bytes 4718592 | tf_op jit(solution)/shard_map/video_attention/pallas_call | solution.py:185
  413.2 12.6 %video_attention.17._ = bf16[1152,3072]{1,0:T(8,128)(2,1)} custom-call(s32[7]{0:T(128)S(1)} %pad_add_fusion.info, bf16[1152,3072]{1,0:T(8,128)(2,1)} %q.23, bf16[1152,3072]{1,0:T(8,128)(2,1)} %k.25, bf16[1152,3072]{1,0:T(8,128)(2,1)} %v.25, bf16[2,1152,256]{2,1,0:T(8,128)(2,1)} %collective-permute-done.12.before, ...), custom_call_target="tpu_custom_call", output_to_operand_aliasing={{}: (8, {})} | custom-call | flops 3019898880 | bytes 4718592 | tf_op jit(solution)/shard_map/video_attention/pallas_call | solution.py:185
  425.8 4.0 collective-permute-start.2
  431.2 12.6 %video_attention.18._ = bf16[1152,3072]{1,0:T(8,128)(2,1)} custom-call(s32[7]{0:T(128)S(1)} %pad_add_fusion.info, bf16[1152,3072]{1,0:T(8,128)(2,1)} %q.23, bf16[1152,3072]{1,0:T(8,128)(2,1)} %k.25, bf16[1152,3072]{1,0:T(8,128)(2,1)} %v.25, bf16[2,1152,256]{2,1,0:T(8,128)(2,1)} %collective-permute-done.10.before, ...), custom_call_target="tpu_custom_call", output_to_operand_aliasing={{}: (8, {})} | custom-call | flops 3019898880 | bytes 4718592 | tf_op jit(solution)/shard_map/video_attention/pallas_call | solution.py:185
  443.8 4.1 collective-permute-start
  449.2 94.9 %psum.15 = f32[12,256]{1,0:T(8,128)S(1)} all-reduce(f32[12,256]{1,0:T(8,128)S(1)} %bitcast.75), channel_id=1, replica_groups=mesh['wide'=16,'narrow'=2] {'wide'}, use_global_device_ids=true, to_apply=%region_4.0 | all-reduce | flops 3072 | bytes 24576 | tf_op jit(solution)/shard_map/psum | solution.py:294
  544.0 12.6 %video_attention.19._ = bf16[1152,3072]{1,0:T(8,128)(2,1)} custom-call(s32[7]{0:T(128)S(1)} %pad_add_fusion.info, bf16[1152,3072]{1,0:T(8,128)(2,1)} %q.23, bf16[1152,3072]{1,0:T(8,128)(2,1)} %k.25, bf16[1152,3072]{1,0:T(8,128)(2,1)} %v.25, bf16[2,1152,256]{2,1,0:T(8,128)(2,1)} %collective-permute-done.8.before, ...), custom_call_target="tpu_custom_call", output_to_operand_aliasing={{}: (8, {})} | custom-call | flops 3019898880 | bytes 4718592 | tf_op jit(solution)/shard_map/video_attention/pallas_call | solution.py:185
  556.6 12.6 %video_attention.20._ = bf16[1152,3072]{1,0:T(8,128)(2,1)} custom-call(s32[7]{0:T(128)S(1)} %pad_add_fusion.info, bf16[1152,3072]{1,0:T(8,128)(2,1)} %q.23, bf16[1152,3072]{1,0:T(8,128)(2,1)} %k.25, bf16[1152,3072]{1,0:T(8,128)(2,1)} %v.25, bf16[2,1152,256]{2,1,0:T(8,128)(2,1)} %collective-permute-done.6.before, ...), custom_call_target="tpu_custom_call", output_to_operand_aliasing={{}: (8, {})} | custom-call | flops 3019898880 | bytes 4718592 | tf_op jit(solution)/shard_map/video_attention/pallas_call | solution.py:185
  569.3 13.0 %video_attention.21._ = bf16[1152,3072]{1,0:T(8,128)(2,1)} custom-call(s32[7]{0:T(128)S(1)} %pad_add_fusion.info, bf16[1152,3072]{1,0:T(8,128)(2,1)} %q.23, bf16[1152,3072]{1,0:T(8,128)(2,1)} %k.25, bf16[1152,3072]{1,0:T(8,128)(2,1)} %v.25, bf16[2,1152,256]{2,1,0:T(8,128)(2,1)} %collective-permute-done.4.before, ...), custom_call_target="tpu_custom_call", output_to_operand_aliasing={{}: (8, {})} | custom-call | flops 3019898880 | bytes 4718592 | tf_op jit(solution)/shard_map/video_attention/pallas_call | solution.py:185
  582.3 12.6 %video_attention.22._ = bf16[1152,3072]{1,0:T(8,128)(2,1)} custom-call(s32[7]{0:T(128)S(1)} %pad_add_fusion.info, bf16[1152,3072]{1,0:T(8,128)(2,1)} %q.23, bf16[1152,3072]{1,0:T(8,128)(2,1)} %k.25, bf16[1152,3072]{1,0:T(8,128)(2,1)} %v.25, bf16[2,1152,256]{2,1,0:T(8,128)(2,1)} %collective-permute-done.2.before, ...), custom_call_target="tpu_custom_call", output_to_operand_aliasing={{}: (8, {})} | custom-call | flops 3019898880 | bytes 4718592 | tf_op jit(solution)/shard_map/video_attention/pallas_call | solution.py:185
  594.9 12.9 %video_attention.23 = bf16[1152,3072]{1,0:T(8,128)(2,1)} custom-call(s32[7]{0:T(128)S(1)} %pad_add_fusion.info, bf16[1152,3072]{1,0:T(8,128)(2,1)} %q.23, bf16[1152,3072]{1,0:T(8,128)(2,1)} %k.25, bf16[1152,3072]{1,0:T(8,128)(2,1)} %v.25, bf16[2,1152,256]{2,1,0:T(8,128)(2,1)} %collective-permute-done.before, ...), custom_call_target="tpu_custom_call", output_to_operand_aliasing={{}: (8, {})} | custom-call | flops 3019898880 | bytes 4718592 | tf_op jit(solution)/shard_map/video_attention/pallas_call | solution.py:185
  607.8 53.6 %all-reduce.3.cloned.1.call-done = f32[12,128,256]{2,1,0:T(8,128)} async-done(((f32[12,128,256]{2,1,0:T(8,128)}), f32[12,128,256]{2,1,0:T(8,128)}) %all-reduce.3.cloned.1.call-update) | async-done | bytes 1572880 | tf_op jit(solution)/shard_map/psum | solution.py:294
  (149 shorter events, 48.1 us)
Async XLA Ops:
  7.2 68.9 %all-gather.2.cloned.1.call-start = ((), (), s32[]{:S(2)}) async-start(), calls=%async_computation.1 | async-start | bytes 7077888 | tf_op jit(solution)/shard_map/all_gather | solution.py:277
  10.5 558.8 %reduce-scatter.2.cloned.1.call-start = ((), (), s32[]{:S(2)}) async-start(), calls=%async_computation.2 | async-start | bytes 4718592 | tf_op jit(solution)/shard_map/reduce_scatter | solution.py:291
  155.4 506.0 %all-reduce.3.cloned.1.call-start = ((), (), s32[]{:S(2)}) async-start(), calls=%async_computation.3 | async-start | bytes 3145728 | tf_op jit(solution)/shard_map/psum | solution.py:294
  156.9 14.5 %collective-permute-start.22 = (bf16[2,1152,256]{2,1,0:T(8,128)(2,1)S(1)}, bf16[2,1152,256]{2,1,0:T(8,128)(2,1)S(1)}, u32[]{:S(2)}, u32[]{:S(2)}) collective-permute-start(bf16[2,1152,256]{2,1,0:T(8,128)(2,1)S(1)} %pad_maximum_fusion.12), channel_id=1, source_target_pairs={{0,2},{2,4},{4,6},{6,8},{8,10},{10,12},{12,14},{14,16},{16,18},{18... | collective-permute-start | bytes 3538952 | tf_op jit(solution)/shard_map/ppermute | solution.py:286
  158.3 15.5 %collective-permute-start.23 = (bf16[2,1152,256]{2,1,0:T(8,128)(2,1)S(1)}, bf16[2,1152,256]{2,1,0:T(8,128)(2,1)S(1)}, u32[]{:S(2)}, u32[]{:S(2)}) collective-permute-start(bf16[2,1152,256]{2,1,0:T(8,128)(2,1)S(1)} %pad_maximum_fusion.12), channel_id=1, source_target_pairs={{2,0},{4,2},{6,4},{8,6},{10,8},{12,10},{14,12},{16,14},{18,16},{20... | collective-permute-start | bytes 3538952 | tf_op jit(solution)/shard_map/ppermute | solution.py:286
  159.8 59.6 %collective-permute-start.20 = (bf16[2,1152,256]{2,1,0:T(8,128)(2,1)S(1)}, bf16[2,1152,256]{2,1,0:T(8,128)(2,1)S(1)}, u32[]{:S(2)}, u32[]{:S(2)}) collective-permute-start(bf16[2,1152,256]{2,1,0:T(8,128)(2,1)S(1)} %pad_maximum_fusion.11), channel_id=1, source_target_pairs={{0,2},{2,4},{4,6},{6,8},{8,10},{10,12},{12,14},{14,16},{16,18},{18... | collective-permute-start | bytes 3538952 | tf_op jit(solution)/shard_map/ppermute | solution.py:286
  165.4 55.2 %collective-permute-start.21 = (bf16[2,1152,256]{2,1,0:T(8,128)(2,1)S(1)}, bf16[2,1152,256]{2,1,0:T(8,128)(2,1)S(1)}, u32[]{:S(2)}, u32[]{:S(2)}) collective-permute-start(bf16[2,1152,256]{2,1,0:T(8,128)(2,1)S(1)} %pad_maximum_fusion.11), channel_id=1, source_target_pairs={{2,0},{4,2},{6,4},{8,6},{10,8},{12,10},{14,12},{16,14},{18,16},{20... | collective-permute-start | bytes 3538952 | tf_op jit(solution)/shard_map/ppermute | solution.py:286
  166.9 64.8 %collective-permute-start.18 = (bf16[2,1152,256]{2,1,0:T(8,128)(2,1)S(1)}, bf16[2,1152,256]{2,1,0:T(8,128)(2,1)S(1)}, u32[]{:S(2)}, u32[]{:S(2)}) collective-permute-start(bf16[2,1152,256]{2,1,0:T(8,128)(2,1)S(1)} %pad_maximum_fusion.10), channel_id=1, source_target_pairs={{0,2},{2,4},{4,6},{6,8},{8,10},{10,12},{12,14},{14,16},{16,18},{18... | collective-permute-start | bytes 3538952 | tf_op jit(solution)/shard_map/ppermute | solution.py:286
  171.3 46.9 %copy-start.30 = (bf16[1,1152,256]{2,1,0:T(8,128)(2,1)S(1)}, bf16[1,1152,256]{2,1,0:T(8,128)(2,1)}, u32[]{:S(2)}) copy-start(bf16[1,1152,256]{2,1,0:T(8,128)(2,1)} %get-tuple-element.18) | copy-start | bytes 1769476
  171.3 46.9 %copy-start.31 = (bf16[1,1152,256]{2,1,0:T(8,128)(2,1)S(1)}, bf16[1,1152,256]{2,1,0:T(8,128)(2,1)}, u32[]{:S(2)}) copy-start(bf16[1,1152,256]{2,1,0:T(8,128)(2,1)} %get-tuple-element.30) | copy-start | bytes 1769476
  172.5 61.6 %collective-permute-start.19 = (bf16[2,1152,256]{2,1,0:T(8,128)(2,1)S(1)}, bf16[2,1152,256]{2,1,0:T(8,128)(2,1)S(1)}, u32[]{:S(2)}, u32[]{:S(2)}) collective-permute-start(bf16[2,1152,256]{2,1,0:T(8,128)(2,1)S(1)} %pad_maximum_fusion.10), channel_id=1, source_target_pairs={{2,0},{4,2},{6,4},{8,6},{10,8},{12,10},{14,12},{16,14},{18,16},{20... | collective-permute-start | bytes 3538952 | tf_op jit(solution)/shard_map/ppermute | solution.py:286
  174.8 81.4 %collective-permute-start.16 = (bf16[2,1152,256]{2,1,0:T(8,128)(2,1)S(1)}, bf16[2,1152,256]{2,1,0:T(8,128)(2,1)S(1)}, u32[]{:S(2)}, u32[]{:S(2)}) collective-permute-start(bf16[2,1152,256]{2,1,0:T(8,128)(2,1)S(1)} %pad_maximum_fusion.9), channel_id=1, source_target_pairs={{0,2},{2,4},{4,6},{6,8},{8,10},{10,12},{12,14},{14,16},{16,18},{18... | collective-permute-start | bytes 3538952 | tf_op jit(solution)/shard_map/ppermute | solution.py:286
  219.4 39.3 %collective-permute-start.17 = (bf16[2,1152,256]{2,1,0:T(8,128)(2,1)S(1)}, bf16[2,1152,256]{2,1,0:T(8,128)(2,1)S(1)}, u32[]{:S(2)}, u32[]{:S(2)}) collective-permute-start(bf16[2,1152,256]{2,1,0:T(8,128)(2,1)S(1)} %pad_maximum_fusion.9), channel_id=1, source_target_pairs={{2,0},{4,2},{6,4},{8,6},{10,8},{12,10},{14,12},{16,14},{18,16},{20... | collective-permute-start | bytes 3538952 | tf_op jit(solution)/shard_map/ppermute | solution.py:286
  220.7 73.5 %collective-permute-start.14 = (bf16[2,1152,256]{2,1,0:T(8,128)(2,1)}, bf16[2,1152,256]{2,1,0:T(8,128)(2,1)S(1)}, u32[]{:S(2)}, u32[]{:S(2)}) collective-permute-start(bf16[2,1152,256]{2,1,0:T(8,128)(2,1)} %pad_maximum_fusion.8), channel_id=1, source_target_pairs={{0,2},{2,4},{4,6},{6,8},{8,10},{10,12},{12,14},{14,16},{16,18},{18... | collective-permute-start | bytes 3538952 | tf_op jit(solution)/shard_map/ppermute | solution.py:286
  231.7 69.9 %collective-permute-start.15 = (bf16[2,1152,256]{2,1,0:T(8,128)(2,1)}, bf16[2,1152,256]{2,1,0:T(8,128)(2,1)}, u32[]{:S(2)}, u32[]{:S(2)}) collective-permute-start(bf16[2,1152,256]{2,1,0:T(8,128)(2,1)} %pad_maximum_fusion.8), channel_id=1, source_target_pairs={{2,0},{4,2},{6,4},{8,6},{10,8},{12,10},{14,12},{16,14},{18,16},{20... | collective-permute-start | bytes 3538952 | tf_op jit(solution)/shard_map/ppermute | solution.py:286
  234.1 106.8 %collective-permute-start.12 = (bf16[2,1152,256]{2,1,0:T(8,128)(2,1)}, bf16[2,1152,256]{2,1,0:T(8,128)(2,1)}, u32[]{:S(2)}, u32[]{:S(2)}) collective-permute-start(bf16[2,1152,256]{2,1,0:T(8,128)(2,1)} %pad_maximum_fusion.7), channel_id=1, source_target_pairs={{0,2},{2,4},{4,6},{6,8},{8,10},{10,12},{12,14},{14,16},{16,18},{18... | collective-permute-start | bytes 3538952 | tf_op jit(solution)/shard_map/ppermute | solution.py:286
  256.2 86.1 %collective-permute-start.13 = (bf16[2,1152,256]{2,1,0:T(8,128)(2,1)}, bf16[2,1152,256]{2,1,0:T(8,128)(2,1)}, u32[]{:S(2)}, u32[]{:S(2)}) collective-permute-start(bf16[2,1152,256]{2,1,0:T(8,128)(2,1)} %pad_maximum_fusion.7), channel_id=1, source_target_pairs={{2,0},{4,2},{6,4},{8,6},{10,8},{12,10},{14,12},{16,14},{18,16},{20... | collective-permute-start | bytes 3538952 | tf_op jit(solution)/shard_map/ppermute | solution.py:286
  257.6 37.9 %copy-start.20 = (bf16[1,1152,256]{2,1,0:T(8,128)(2,1)S(1)}, bf16[1,1152,256]{2,1,0:T(8,128)(2,1)}, u32[]{:S(2)}) copy-start(bf16[1,1152,256]{2,1,0:T(8,128)(2,1)} %get-tuple-element.23) | copy-start | bytes 1769476
  257.6 37.9 %copy-start.21 = (bf16[1,1152,256]{2,1,0:T(8,128)(2,1)S(1)}, bf16[1,1152,256]{2,1,0:T(8,128)(2,1)}, u32[]{:S(2)}) copy-start(bf16[1,1152,256]{2,1,0:T(8,128)(2,1)} %get-tuple-element.35) | copy-start | bytes 1769476
  258.7 38.0 %copy-start.14 = (bf16[2,1152,256]{2,1,0:T(8,128)(2,1)}, bf16[2,1152,256]{2,1,0:T(8,128)(2,1)S(1)}, u32[]{:S(2)}) copy-start(bf16[2,1152,256]{2,1,0:T(8,128)(2,1)S(1)} %collective-permute-done.17.after) | copy-start | bytes 3538948
  258.7 100.9 %collective-permute-start.10 = (bf16[2,1152,256]{2,1,0:T(8,128)(2,1)}, bf16[2,1152,256]{2,1,0:T(8,128)(2,1)}, u32[]{:S(2)}, u32[]{:S(2)}) collective-permute-start(bf16[2,1152,256]{2,1,0:T(8,128)(2,1)} %pad_maximum_fusion.6), channel_id=1, source_target_pairs={{0,2},{2,4},{4,6},{6,8},{8,10},{10,12},{12,14},{14,16},{16,18},{18... | collective-permute-start | bytes 3538952 | tf_op jit(solution)/shard_map/ppermute | solution.py:286
  294.2 66.7 %collective-permute-start.11 = (bf16[2,1152,256]{2,1,0:T(8,128)(2,1)}, bf16[2,1152,256]{2,1,0:T(8,128)(2,1)}, u32[]{:S(2)}, u32[]{:S(2)}) collective-permute-start(bf16[2,1152,256]{2,1,0:T(8,128)(2,1)} %pad_maximum_fusion.6), channel_id=1, source_target_pairs={{2,0},{4,2},{6,4},{8,6},{10,8},{12,10},{14,12},{16,14},{18,16},{20... | collective-permute-start | bytes 3538952 | tf_op jit(solution)/shard_map/ppermute | solution.py:286
  301.6 110.2 %collective-permute-start.8 = (bf16[2,1152,256]{2,1,0:T(8,128)(2,1)}, bf16[2,1152,256]{2,1,0:T(8,128)(2,1)}, u32[]{:S(2)}, u32[]{:S(2)}) collective-permute-start(bf16[2,1152,256]{2,1,0:T(8,128)(2,1)} %pad_maximum_fusion.5), channel_id=1, source_target_pairs={{0,2},{2,4},{4,6},{6,8},{8,10},{10,12},{12,14},{14,16},{16,18},{18... | collective-permute-start | bytes 3538952 | tf_op jit(solution)/shard_map/ppermute | solution.py:286
  340.9 84.9 %collective-permute-start.9 = (bf16[2,1152,256]{2,1,0:T(8,128)(2,1)}, bf16[2,1152,256]{2,1,0:T(8,128)(2,1)}, u32[]{:S(2)}, u32[]{:S(2)}) collective-permute-start(bf16[2,1152,256]{2,1,0:T(8,128)(2,1)} %pad_maximum_fusion.5), channel_id=1, source_target_pairs={{2,0},{4,2},{6,4},{8,6},{10,8},{12,10},{14,12},{16,14},{18,16},{20... | collective-permute-start | bytes 3538952 | tf_op jit(solution)/shard_map/ppermute | solution.py:286
  342.4 87.5 %collective-permute-start.6 = (bf16[2,1152,256]{2,1,0:T(8,128)(2,1)}, bf16[2,1152,256]{2,1,0:T(8,128)(2,1)}, u32[]{:S(2)}, u32[]{:S(2)}) collective-permute-start(bf16[2,1152,256]{2,1,0:T(8,128)(2,1)} %pad_maximum_fusion.4), channel_id=1, source_target_pairs={{0,2},{2,4},{4,6},{6,8},{8,10},{10,12},{12,14},{14,16},{16,18},{18... | collective-permute-start | bytes 3538952 | tf_op jit(solution)/shard_map/ppermute | solution.py:286
  359.6 84.1 %collective-permute-start.7 = (bf16[2,1152,256]{2,1,0:T(8,128)(2,1)}, bf16[2,1152,256]{2,1,0:T(8,128)(2,1)}, u32[]{:S(2)}, u32[]{:S(2)}) collective-permute-start(bf16[2,1152,256]{2,1,0:T(8,128)(2,1)} %pad_maximum_fusion.4), channel_id=1, source_target_pairs={{2,0},{4,2},{6,4},{8,6},{10,8},{12,10},{14,12},{16,14},{18,16},{20... | collective-permute-start | bytes 3538952 | tf_op jit(solution)/shard_map/ppermute | solution.py:286
  360.9 86.9 %collective-permute-start.4 = (bf16[2,1152,256]{2,1,0:T(8,128)(2,1)}, bf16[2,1152,256]{2,1,0:T(8,128)(2,1)}, u32[]{:S(2)}, u32[]{:S(2)}) collective-permute-start(bf16[2,1152,256]{2,1,0:T(8,128)(2,1)} %pad_maximum_fusion.3), channel_id=1, source_target_pairs={{0,2},{2,4},{4,6},{6,8},{8,10},{10,12},{12,14},{14,16},{16,18},{18... | collective-permute-start | bytes 3538952 | tf_op jit(solution)/shard_map/ppermute | solution.py:286
  411.8 157.5 %collective-permute-start.5 = (bf16[2,1152,256]{2,1,0:T(8,128)(2,1)}, bf16[2,1152,256]{2,1,0:T(8,128)(2,1)}, u32[]{:S(2)}, u32[]{:S(2)}) collective-permute-start(bf16[2,1152,256]{2,1,0:T(8,128)(2,1)} %pad_maximum_fusion.3), channel_id=1, source_target_pairs={{2,0},{4,2},{6,4},{8,6},{10,8},{12,10},{14,12},{16,14},{18,16},{20... | collective-permute-start | bytes 3538952 | tf_op jit(solution)/shard_map/ppermute | solution.py:286
  425.8 156.4 %collective-permute-start.2 = (bf16[2,1152,256]{2,1,0:T(8,128)(2,1)}, bf16[2,1152,256]{2,1,0:T(8,128)(2,1)}, u32[]{:S(2)}, u32[]{:S(2)}) collective-permute-start(bf16[2,1152,256]{2,1,0:T(8,128)(2,1)} %pad_maximum_fusion.2), channel_id=1, source_target_pairs={{0,2},{2,4},{4,6},{6,8},{8,10},{10,12},{12,14},{14,16},{16,18},{18... | collective-permute-start | bytes 3538952 | tf_op jit(solution)/shard_map/ppermute | solution.py:286
  429.9 152.4 %collective-permute-start.3 = (bf16[2,1152,256]{2,1,0:T(8,128)(2,1)}, bf16[2,1152,256]{2,1,0:T(8,128)(2,1)}, u32[]{:S(2)}, u32[]{:S(2)}) collective-permute-start(bf16[2,1152,256]{2,1,0:T(8,128)(2,1)} %pad_maximum_fusion.2), channel_id=1, source_target_pairs={{2,0},{4,2},{6,4},{8,6},{10,8},{12,10},{14,12},{16,14},{18,16},{20... | collective-permute-start | bytes 3538952 | tf_op jit(solution)/shard_map/ppermute | solution.py:286
  443.8 151.1 %collective-permute-start = (bf16[2,1152,256]{2,1,0:T(8,128)(2,1)}, bf16[2,1152,256]{2,1,0:T(8,128)(2,1)}, u32[]{:S(2)}, u32[]{:S(2)}) collective-permute-start(bf16[2,1152,256]{2,1,0:T(8,128)(2,1)} %pad_maximum_fusion.1), channel_id=1, source_target_pairs={{0,2},{2,4},{4,6},{6,8},{8,10},{10,12},{12,14},{14,16},{16,18},{18... | collective-permute-start | bytes 3538952 | tf_op jit(solution)/shard_map/ppermute | solution.py:286
  447.8 147.1 %collective-permute-start.1 = (bf16[2,1152,256]{2,1,0:T(8,128)(2,1)}, bf16[2,1152,256]{2,1,0:T(8,128)(2,1)}, u32[]{:S(2)}, u32[]{:S(2)}) collective-permute-start(bf16[2,1152,256]{2,1,0:T(8,128)(2,1)} %pad_maximum_fusion.1), channel_id=1, source_target_pairs={{2,0},{4,2},{6,4},{8,6},{10,8},{12,10},{14,12},{16,14},{18,16},{20... | collective-permute-start | bytes 3538952 | tf_op jit(solution)/shard_map/ppermute | solution.py:286
  (35 other events, 326.5 us)
Sparse Core Ops, SparseCore 0:
  10.6 65.3 all-gather.1
  155.5 43.7 reduce-scatter.1
  569.4 91.9 all-reduce.2
